TPU v7x, 512 devices: a whole 4x8x8 slice. The times are simulated.
512 devices in a mesh: tmpl: 32 (over z, y_lo), sta: 16 (over y_hi, x, core).
Axes of the slice: x: 4, y: 8 (y_hi: 2, y_lo: 4; y = y_hi * 4 + y_lo), z: 8, core: 2. Of those that a mesh axis runs over, the one named last changes fastest.
Arguments:
- waveform: bfloat16 [1200, 5120], P('sta', 'tmpl'), may hold values from -40 to 40
- templates: bfloat16 [1024, 30, 400], P('tmpl'), may hold values from -5 to 5
- channel: int32 [1024, 30], P('tmpl'), may hold values from 0 to 1199, as said below
- moveout: int32 [1024, 30], P('tmpl'), may hold values from 0 to 399
Outputs:
- detection: float32 [1024, 4096], P('tmpl', 'sta')
Inputs may be any that keep to these rules, and one draw needn't show every extreme that they name: `channel`: each template lists 30 distinct channels, the three components 3 q, 3 q + 1, 3 q + 2 of 10 stations q, in any slot order. Call the channels c with equal c // 75 a station group. A template's channels lie in two station groups g and (g + 1) modulo the number of groups, 15 in each. Among the 32 templates of one aligned block of rows, at most 150 entries fall into one station group, and exactly 150 into some group.
All inputs are finite; a program needn't handle non-finite values.
Results may differ from a plain program's by a relative error of at most 0.0029.
Values may be sent and summed in bfloat16 or wider, within the bound.
A program may use at most 64 MiB of HBM per device.

v0:
```python
import math

import jax
import jax.numpy as jnp
from jax import lax
from jax.experimental import pallas as pl
from jax.experimental.pallas import tpu as pltpu
from jax.sharding import PartitionSpec as P

F32, BF16, I32 = jnp.float32, jnp.bfloat16, jnp.int32
TAPS = 400
LANES = 128
HALF = 64
WIDE = 512
CH, CHP = 75, 80
PITCH = 84
ROWS = 40
USED = 36
PICK, SLOT = 10, 15
Z, Y, CHUNK = 8, 4, 5
GROUPS = 16
BATCH, EACH = 2, 5


def nt(a, b):
    return lax.dot_general(a, b, (((1,), (1,)), ((), ())), preferred_element_type=F32)


def nn(a, b):
    return jnp.dot(a, b, preferred_element_type=F32)


def iota(shape, d):
    return lax.broadcasted_iota(I32, shape, d)


def ones_where(cond):
    return jnp.where(cond, 1.0, 0.0).astype(BF16)


def pair_lists(first, chan, move):
    n, s = chan.shape
    inside = (chan >= first) & (chan < first + CH)
    loc = ones_where(inside)
    slot_rank = nn(loc, ones_where(iota((s, s), 0) < iota((s, s), 1)))
    count = nt(jnp.ones((16, s), BF16), loc)
    rank = nn(ones_where(count > 0.5), ones_where(iota((n, n), 0) < iota((n, n), 1))).astype(I32)
    sel = ones_where((rank == iota((16, n), 0)) & (count > 0.5))

    def keep(v):
        return nn(sel, jnp.where(inside, v, 0).astype(F32).astype(BF16))

    cols = (keep(chan - first), keep(move // LANES), keep(move % LANES), keep(iota((n, s), 0)))
    lsel = nn(sel, loc)
    rsel = nn(sel, slot_rank.astype(BF16)).astype(I32)
    eq = (rsel[:, None, :] == iota((16, 16, s), 1)) & (lsel[:, None, :] > 0.5)
    eq3 = jnp.where(eq, 1.0, 0.0)
    eq = eq3.reshape(256, s).astype(BF16)
    diag = iota((16, 256), 0) == iota((16, 256), 1) // 16
    rows = []
    for v in cols:
        rows.append(jnp.sum(jnp.where(diag, nt(v.astype(BF16), eq), 0.0), axis=0, keepdims=True))
    place = jnp.sum(eq3 * (iota((16, 16, s), 2).astype(F32) * n + cols[3][:, None, :] + 1.0), axis=2, keepdims=True)
    return jnp.concatenate(rows + rows, axis=0).astype(I32), place.reshape(256, 1) - 1.0


def combine_rows(chan, half):
    n = chan.shape[0]
    grp = chan // CH
    low = jnp.min(grp, axis=1, keepdims=True)
    high = jnp.max(grp, axis=1, keepdims=True)
    lane = iota((n, BATCH * 256), 1)
    batch, group, part, row = lane // 256, lane % 256 // 16, lane % 16 // 8, lane % 8
    here = (group == low) | (group == high)
    rank = nn(ones_where(iota((n, n), 1) < iota((n, n), 0)), ones_where(here)).astype(I32)
    hit = here & (part == half) & (row < EACH) & (rank == batch * EACH + row)
    return jnp.where(hit, 1.0, 0.0)


def kernel(w_ref, t_hbm, ch_ref, mv_ref, o_ref,
           wide, ybuf, x_all, t_ref, scal_v, scal, units, band, xs, sqs, frames, lev, rolled, outbox, inbox,
           y_send, y_recv, z_send, z_recv, a_send, a_recv, t_sem, s_sem):
    tm, st = lax.axis_index("tmpl"), lax.axis_index("sta")
    zz, yy = tm // Y, tm % Y
    up, down = (tm + Y) % (Z * Y), (tm + Z * Y - Y) % (Z * Y)
    y_peer = [zz * Y + (yy + d) % Y for d in range(1, Y)]
    s_peer = [(st + d) % GROUPS for d in range(1, GROUPS)]

    barrier = pltpu.get_barrier_semaphore()
    for p in y_peer + [up, down]:
        pl.semaphore_signal(barrier, inc=1, device_id={"tmpl": p}, device_id_type=pl.DeviceIdType.MESH)
    for p in s_peer:
        pl.semaphore_signal(barrier, inc=1, device_id={"sta": p}, device_id_type=pl.DeviceIdType.MESH)

    t_copy = pltpu.make_async_copy(t_hbm, t_ref, t_sem)
    t_copy.start()

    wide[...] = jnp.zeros_like(wide)
    wide[pl.ds(0, CH), pl.ds(0, 160)] = w_ref[...].astype(F32)
    own = pltpu.roll(wide[...], 32 * yy, 1)
    own = jnp.concatenate([own[:, :LANES], own[:, LANES:]], axis=0).astype(BF16)
    ybuf[yy] = own
    outbox[...] = jnp.zeros_like(outbox)

    pl.semaphore_wait(barrier, Y - 1 + 2 + GROUPS - 1)

    y_copies = []
    for d in range(1, Y):
        cp = pltpu.make_async_remote_copy(
            src_ref=ybuf.at[yy], dst_ref=ybuf.at[yy], send_sem=y_send.at[d - 1], recv_sem=y_recv.at[d - 1],
            device_id={"tmpl": y_peer[d - 1]}, device_id_type=pl.DeviceIdType.MESH)
        cp.start()
        y_copies.append(cp)

    sc, place = pair_lists(st * CH, ch_ref[...], mv_ref[...])
    scal_v[...] = sc
    s_copy = pltpu.make_async_copy(scal_v, scal, s_sem)
    s_copy.start()

    for cp in y_copies:
        cp.wait()
    parts = [ybuf[y].astype(F32) for y in range(Y)]
    for n in range(CHUNK):
        v = 0.0
        if n < Y:
            v += parts[n][:CHP]
        if n > 0:
            v += parts[n - 1][CHP:]
        x_all[zz * CHUNK + n] = v.astype(BF16)

    def ring(step, direction):
        src = (zz + Z - step) % Z if direction == 0 else (zz + step) % Z
        first, count = (0, CHUNK) if step < 3 else ((0, 3) if direction == 0 else (3, 2))
        piece = x_all.at[pl.ds(src * CHUNK + first, count)]
        return pltpu.make_async_remote_copy(
            src_ref=piece, dst_ref=piece, send_sem=z_send.at[direction, step], recv_sem=z_recv.at[direction, step],
            device_id={"tmpl": up if direction == 0 else down}, device_id_type=pl.DeviceIdType.MESH)

    steps = [[ring(s, d) for d in range(2)] for s in range(4)]
    for cp in steps[0]:
        cp.start()

    t_copy.wait()
    s_copy.wait()

    slots, count = t_ref.shape[:2]
    rows = t_ref[...].reshape(slots * count, TAPS)
    pick = nn(ones_where(place[:16 * PICK].astype(I32) == iota((16 * PICK, slots * count), 1)), rows)
    unit = pick / jnp.sqrt(jnp.sum(pick * pick, axis=1, keepdims=True) / TAPS + 1e-5)
    unit = unit.astype(BF16).astype(F32)
    units[...] = jnp.concatenate([unit, jnp.zeros((16 * PICK, WIDE - TAPS), F32)], axis=1)

    def bands(lo, hi):
        @pl.loop(lo, hi)
        def _(i):
            unit = units[pl.ds(pl.multiple_of(i * 16, 16), 16), :]
            for j in range(SLOT):
                row = jnp.broadcast_to(unit[j:j + 1, :], (HALF, WIDE))
                band[i * SLOT + j] = pltpu.roll(row, 0, 1, stride=1, stride_axis=0).astype(BF16)

    cuts = (0, 3, 6, 9, 10)
    for s in range(4):
        bands(cuts[s], cuts[s + 1])
        for d in range(2):
            steps[s][d].wait()
            if s < 3:
                steps[s + 1][d].start()

    lane = iota((CHP, LANES), 1)

    @pl.loop(0, Z)
    def _(z):
        rows = [x_all[z * CHUNK + n] for n in range(CHUNK)] + [x_all[jnp.minimum(z * CHUNK + CHUNK, ROWS - 1)]]
        rows = [v.astype(F32) for v in rows]
        for n in range(CHUNK):
            g = z * CHUNK + n
            xs[pl.ds(g * PITCH, CHP), :] = rows[n]
            xs[pl.ds((ROWS + 4 + g) * PITCH, CHP), :] = pltpu.roll(jnp.where(lane < HALF, rows[n + 1], rows[n]), HALF, 1)
            sqs[pl.ds(pl.multiple_of(g * CHP, CHP), CHP), :] = (rows[n] * rows[n]).astype(BF16)

    e, d = iota((5 * LANES, LANES), 0), iota((5 * LANES, LANES), 1)
    window = ones_where((e >= d) & (e < d + TAPS))
    factor = 1.0 / math.sqrt(TAPS * 2 * SLOT)
    many = 9

    @pl.loop(0, USED // many)
    def _(t):
        base = t * (many * CHP)
        s = 0.0
        for q in range(5):
            rows = sqs[pl.ds(pl.multiple_of(base + q * CHP, CHP), many * CHP), :]
            s += nn(rows, window[q * LANES:(q + 1) * LANES])
        s = lax.rsqrt(s / TAPS + 1e-5) * factor
        for n in range(many):
            lev[pl.ds((t * many + n) * PITCH, CHP), :] = s[n * CHP:(n + 1) * CHP]

    @pl.loop(0, CH)
    def _(c):
        for h in range(2):
            for q in range(4):
                v = xs[pl.ds(c + (h * (ROWS + 4) + q) * PITCH, ROWS, stride=PITCH), :]
                frames[c, pl.ds(h * ROWS, ROWS), pl.ds(q * LANES, LANES)] = v.astype(BF16)

    lane32 = iota((32, LANES), 1)

    def stacks(b):
        @pl.loop(0, EACH)
        def _(ii):
            i = b * EACH + ii
            acc = jnp.zeros((32, LANES), F32)
            for j in range(SLOT):
                p = i * 16 + j
                c, a, r = (jnp.clip(scal[n, p], 0, top) for n, top in enumerate((CH - 1, 3, LANES - 1)))
                y = nt(frames[c], band[i * SLOT + j])
                y = jnp.concatenate([y[:ROWS], y[ROWS:]], axis=1)
                rolled[j] = pltpu.roll(y * lev[pl.ds(c, ROWS, stride=PITCH), :], (LANES - r) % LANES, 1)
                acc += jnp.where(lane32 < LANES - r, rolled[j, pl.ds(a, 32), :], rolled[j, pl.ds(a + 1, 32), :])
            outbox[b, pl.ds(ii, 32, stride=8), :] = acc

    sends = []
    for b in range(BATCH):
        stacks(b)
        for d in range(1, GROUPS):
            cp = pltpu.make_async_remote_copy(
                src_ref=outbox.at[b, pl.ds(s_peer[d - 1] * 16, 16)], dst_ref=inbox.at[b, pl.ds(st * 16, 16)],
                send_sem=a_send.at[b, d - 1], recv_sem=a_recv.at[b, d - 1],
                device_id={"sta": s_peer[d - 1]}, device_id_type=pl.DeviceIdType.MESH)
            cp.start()
            sends.append(cp)
        inbox[b, pl.ds(st * 16, 16), :] = outbox[b, pl.ds(st * 16, 16), :]

    hits = [combine_rows(ch_ref[...], h) for h in range(2)]
    for cp in sends:
        cp.wait()
    rows = inbox[...].reshape(BATCH * 256, LANES)
    for h in range(2):
        o_ref[:, pl.ds(h * LANES, LANES)] = jnp.dot(
            hits[h], rows, precision=lax.Precision.HIGHEST, preferred_element_type=F32)


def shards(waveform, templates, channel, moveout):
    vm = pl.BlockSpec(memory_space=pltpu.VMEM)
    sem = pltpu.SemaphoreType.DMA
    templates = templates.transpose(1, 0, 2)
    return pl.pallas_call(
        kernel,
        out_shape=jax.ShapeDtypeStruct((templates.shape[1], 2 * LANES), F32),
        in_specs=[vm, pl.BlockSpec(memory_space=pl.ANY), vm, vm],
        out_specs=vm,
        scratch_shapes=[
            pltpu.VMEM((CHP, 2 * LANES), F32),
            pltpu.VMEM((Y, 2 * CHP, LANES), BF16),
            pltpu.VMEM((ROWS, CHP, LANES), BF16),
            pltpu.VMEM(templates.shape, BF16),
            pltpu.VMEM((8, 256), I32),
            pltpu.SMEM((8, 256), I32),
            pltpu.VMEM((16 * PICK, WIDE), F32),
            pltpu.VMEM((PICK * SLOT, HALF, WIDE), BF16),
            pltpu.VMEM((2 * (ROWS + 4) * PITCH + CHP, LANES), F32),
            pltpu.VMEM((ROWS * CHP, LANES), BF16),
            pltpu.VMEM((CHP, 2 * ROWS, WIDE), BF16),
            pltpu.VMEM((ROWS * PITCH + CHP, LANES), F32),
            pltpu.VMEM((SLOT, ROWS, LANES), F32),
            pltpu.VMEM((BATCH, 264, LANES), F32),
            pltpu.VMEM((BATCH, 256, LANES), F32),
            sem((Y - 1,)), sem((Y - 1,)), sem((2, 4)), sem((2, 4)),
            sem((BATCH, GROUPS - 1)), sem((BATCH, GROUPS - 1)), sem(()), sem(()),
        ],
        compiler_params=pltpu.CompilerParams(
            vmem_limit_bytes=56 << 20, collective_id=0, has_side_effects=True
        ),
    )(waveform, templates, channel, moveout)


def solution(mesh):
    placed = (P("sta", "tmpl"), P("tmpl", None, None), P("tmpl", None), P("tmpl", None))
    return jax.shard_map(
        shards, mesh=mesh, in_specs=placed, out_specs=P("tmpl", "sta"), check_vma=False
    )
```

profile of v0, /device:TPU:1, one launch (start us, length us, event | category | flops | bytes accessed | tf_op | source)
XLA Modules:
  0.0 57.3 jit_solution(5412883286162891639)
XLA Ops:
  0.0 55.9 %shard_map.46 = f32[32,256]{1,0:T(8,128)} custom-call(bf16[75,160]{1,0:T(8,128)(2,1)} %w_ref.1, bf16[30,32,400]{2,1,0:T(8,128)(2,1)} %bitcast.1, s32[32,30]{1,0:T(8,128)} %ch_ref.1, s32[32,30]{1,0:T(8,128)} %mv_ref.1), custom_call_target="tpu_custom_call" | custom-call | tf_op jit(solution)/shard_map/pallas_call | solution.py:245
  55.9 1.4 %copy.6 = f32[32,256]{1,0:T(8,128)} copy(f32[32,256]{1,0:T(8,128)} %shard_map.46) | data formatting | bytes 65536
where the time goes:
time: 57.5 us; the launch traced here: 57.3 us
  Pallas kernels  55.9 us (97%)
  local copies, waits for them, and re-layouts  1.38 us (2%)
    pallas_call x1, Pallas kernels, shards(): pl.pallas_call(kernel, out_shape=jax.ShapeDtypeStruct((templates.shape[1]...  55.9 us
    unnamed x1, local copies, waits for them, and re-layouts  1.38 us

commit v1 on v0

--- a/solution.py
+++ b/solution.py
@@ -15,7 +15,6 @@
 CH, CHP = 75, 80
 PITCH = 84
 ROWS = 40
-USED = 36
 PICK, SLOT = 10, 15
 Z, Y, CHUNK = 8, 4, 5
 GROUPS = 16
@@ -82,12 +81,12 @@
            y_send, y_recv, z_send, z_recv, a_send, a_recv, t_sem, s_sem):
     tm, st = lax.axis_index("tmpl"), lax.axis_index("sta")
     zz, yy = tm // Y, tm % Y
-    up, down = (tm + Y) % (Z * Y), (tm + Z * Y - Y) % (Z * Y)
+    z_peer = {d: (tm + (Z + d) * Y) % (Z * Y) for d in (1, -1, 2, -2)}
     y_peer = [zz * Y + (yy + d) % Y for d in range(1, Y)]
     s_peer = [(st + d) % GROUPS for d in range(1, GROUPS)]
 
     barrier = pltpu.get_barrier_semaphore()
-    for p in y_peer + [up, down]:
+    for p in y_peer + list(z_peer.values()):
         pl.semaphore_signal(barrier, inc=1, device_id={"tmpl": p}, device_id_type=pl.DeviceIdType.MESH)
     for p in s_peer:
         pl.semaphore_signal(barrier, inc=1, device_id={"sta": p}, device_id_type=pl.DeviceIdType.MESH)
@@ -102,7 +101,7 @@
     ybuf[yy] = own
     outbox[...] = jnp.zeros_like(outbox)
 
-    pl.semaphore_wait(barrier, Y - 1 + 2 + GROUPS - 1)
+    pl.semaphore_wait(barrier, Y - 1 + 4 + GROUPS - 1)
 
     y_copies = []
     for d in range(1, Y):
@@ -126,18 +125,21 @@
             v += parts[n][:CHP]
         if n > 0:
             v += parts[n - 1][CHP:]
-        x_all[zz * CHUNK + n] = v.astype(BF16)
-
-    def ring(step, direction):
-        src = (zz + Z - step) % Z if direction == 0 else (zz + step) % Z
-        first, count = (0, CHUNK) if step < 3 else ((0, 3) if direction == 0 else (3, 2))
-        piece = x_all.at[pl.ds(src * CHUNK + first, count)]
+        x_all[n] = v.astype(BF16)
+
+    def pass_on(n, chunk, d, first=0, count=CHUNK):
+        there = (chunk - d) % Z
         return pltpu.make_async_remote_copy(
-            src_ref=piece, dst_ref=piece, send_sem=z_send.at[direction, step], recv_sem=z_recv.at[direction, step],
-            device_id={"tmpl": up if direction == 0 else down}, device_id_type=pl.DeviceIdType.MESH)
-
-    steps = [[ring(s, d) for d in range(2)] for s in range(4)]
-    for cp in steps[0]:
+            src_ref=x_all.at[pl.ds(chunk % Z * CHUNK + first, count)],
+            dst_ref=x_all.at[pl.ds(there * CHUNK + first, count)],
+            send_sem=z_send.at[n], recv_sem=z_recv.at[n],
+            device_id={"tmpl": z_peer[d]}, device_id_type=pl.DeviceIdType.MESH)
+
+    from_two = [pass_on(0, 0, 2), pass_on(1, 0, -2)]
+    from_one = [pass_on(2, 0, 1), pass_on(3, 0, -1)]
+    from_four = [pass_on(4, -2, 2, 0, 3), pass_on(5, 2, -2, 3, 2)]
+    from_three = [pass_on(6, -2, 1), pass_on(7, 2, -1)]
+    for cp in from_two + from_one:
         cp.start()
 
     t_copy.wait()
@@ -158,41 +160,64 @@
                 row = jnp.broadcast_to(unit[j:j + 1, :], (HALF, WIDE))
                 band[i * SLOT + j] = pltpu.roll(row, 0, 1, stride=1, stride_axis=0).astype(BF16)
 
-    cuts = (0, 3, 6, 9, 10)
-    for s in range(4):
-        bands(cuts[s], cuts[s + 1])
-        for d in range(2):
-            steps[s][d].wait()
-            if s < 3:
-                steps[s + 1][d].start()
-
     lane = iota((CHP, LANES), 1)
 
-    @pl.loop(0, Z)
-    def _(z):
-        rows = [x_all[z * CHUNK + n] for n in range(CHUNK)] + [x_all[jnp.minimum(z * CHUNK + CHUNK, ROWS - 1)]]
-        rows = [v.astype(F32) for v in rows]
+    def put(g, row, odd):
+        xs[pl.ds((g + odd * (ROWS + 4)) * PITCH, CHP), :] = row
+
+    def take(c):
+        rows = [x_all[c * CHUNK + n].astype(F32) for n in range(CHUNK)]
         for n in range(CHUNK):
-            g = z * CHUNK + n
-            xs[pl.ds(g * PITCH, CHP), :] = rows[n]
-            xs[pl.ds((ROWS + 4 + g) * PITCH, CHP), :] = pltpu.roll(jnp.where(lane < HALF, rows[n + 1], rows[n]), HALF, 1)
-            sqs[pl.ds(pl.multiple_of(g * CHP, CHP), CHP), :] = (rows[n] * rows[n]).astype(BF16)
+            again = (0, ROWS) if c == 0 and n < 4 else (0,)
+            later = pltpu.roll(jnp.where(lane < HALF, rows[n + 1], rows[n]), HALF, 1) if n < CHUNK - 1 else None
+            square = (rows[n] * rows[n]).astype(BF16)
+            for more in again:
+                g = c * CHUNK + n + more
+                put(g, rows[n], 0)
+                if later is not None:
+                    put(g, later, 1)
+                sqs[pl.ds(g * CHP, CHP), :] = square
 
     e, d = iota((5 * LANES, LANES), 0), iota((5 * LANES, LANES), 1)
     window = ones_where((e >= d) & (e < d + TAPS))
     factor = 1.0 / math.sqrt(TAPS * 2 * SLOT)
-    many = 9
-
-    @pl.loop(0, USED // many)
-    def _(t):
-        base = t * (many * CHP)
+    many = 10
+
+    def levels(g):
         s = 0.0
         for q in range(5):
-            rows = sqs[pl.ds(pl.multiple_of(base + q * CHP, CHP), many * CHP), :]
-            s += nn(rows, window[q * LANES:(q + 1) * LANES])
+            s += nn(sqs[pl.ds((g + q) * CHP, many * CHP), :], window[q * LANES:(q + 1) * LANES])
         s = lax.rsqrt(s / TAPS + 1e-5) * factor
         for n in range(many):
-            lev[pl.ds((t * many + n) * PITCH, CHP), :] = s[n * CHP:(n + 1) * CHP]
+            lev[pl.ds((g + n) * PITCH, CHP), :] = s[n * CHP:(n + 1) * CHP]
+
+    bands(0, 5)
+    for near, far, one in zip(from_two, from_four, from_three):
+        near.wait_recv()
+        far.start()
+        one.start()
+    bands(5, PICK)
+    for c in (0, 2, 6):
+        take(c)
+    for cp in from_one:
+        cp.wait_recv()
+    for c in (1, 7):
+        take(c)
+    levels(0)
+    levels(30)
+    for cp in from_three:
+        cp.wait_recv()
+    for c in (3, 5):
+        take(c)
+    for cp in from_four:
+        cp.wait_recv()
+    take(4)
+    for c in range(Z):
+        g = c * CHUNK + CHUNK - 1
+        first, second = x_all[g].astype(F32), x_all[(g + 1) % ROWS].astype(F32)
+        put(g, pltpu.roll(jnp.where(lane < HALF, second, first), HALF, 1), 1)
+    levels(10)
+    levels(20)
 
     @pl.loop(0, CH)
     def _(c):
@@ -201,6 +226,7 @@
                 v = xs[pl.ds(c + (h * (ROWS + 4) + q) * PITCH, ROWS, stride=PITCH), :]
                 frames[c, pl.ds(h * ROWS, ROWS), pl.ds(q * LANES, LANES)] = v.astype(BF16)
 
+    start = (ROWS - CHUNK * zz) % ROWS
     lane32 = iota((32, LANES), 1)
 
     def stacks(b):
@@ -213,8 +239,11 @@
                 c, a, r = (jnp.clip(scal[n, p], 0, top) for n, top in enumerate((CH - 1, 3, LANES - 1)))
                 y = nt(frames[c], band[i * SLOT + j])
                 y = jnp.concatenate([y[:ROWS], y[ROWS:]], axis=1)
-                rolled[j] = pltpu.roll(y * lev[pl.ds(c, ROWS, stride=PITCH), :], (LANES - r) % LANES, 1)
-                acc += jnp.where(lane32 < LANES - r, rolled[j, pl.ds(a, 32), :], rolled[j, pl.ds(a + 1, 32), :])
+                w = pltpu.roll(y * lev[pl.ds(c, ROWS, stride=PITCH), :], (LANES - r) % LANES, 1)
+                rolled[j, pl.ds(0, ROWS), :] = w
+                rolled[j, pl.ds(ROWS, 32), :] = w[:32]
+                here, after = rolled[j, pl.ds(start + a, 32), :], rolled[j, pl.ds(start + a + 1, 32), :]
+                acc += jnp.where(lane32 < LANES - r, here, after)
             outbox[b, pl.ds(ii, 32, stride=8), :] = acc
 
     sends = []
@@ -230,12 +259,17 @@
         inbox[b, pl.ds(st * 16, 16), :] = outbox[b, pl.ds(st * 16, 16), :]
 
     hits = [combine_rows(ch_ref[...], h) for h in range(2)]
-    for cp in sends:
-        cp.wait()
-    rows = inbox[...].reshape(BATCH * 256, LANES)
+    total = [0.0, 0.0]
+    for b in range(BATCH):
+        for cp in sends[b * (GROUPS - 1):(b + 1) * (GROUPS - 1)]:
+            cp.wait_recv()
+        for h in range(2):
+            total[h] += jnp.dot(hits[h][:, b * 256:(b + 1) * 256], inbox[b],
+                                precision=lax.Precision.HIGHEST, preferred_element_type=F32)
     for h in range(2):
-        o_ref[:, pl.ds(h * LANES, LANES)] = jnp.dot(
-            hits[h], rows, precision=lax.Precision.HIGHEST, preferred_element_type=F32)
+        o_ref[:, pl.ds(h * LANES, LANES)] = total[h]
+    for cp in from_two + from_one + from_four + from_three + sends:
+        cp.wait_send()
 
 
 def shards(waveform, templates, channel, moveout):
@@ -257,13 +291,13 @@
             pltpu.VMEM((16 * PICK, WIDE), F32),
             pltpu.VMEM((PICK * SLOT, HALF, WIDE), BF16),
             pltpu.VMEM((2 * (ROWS + 4) * PITCH + CHP, LANES), F32),
-            pltpu.VMEM((ROWS * CHP, LANES), BF16),
+            pltpu.VMEM(((ROWS + 4) * CHP, LANES), BF16),
             pltpu.VMEM((CHP, 2 * ROWS, WIDE), BF16),
             pltpu.VMEM((ROWS * PITCH + CHP, LANES), F32),
-            pltpu.VMEM((SLOT, ROWS, LANES), F32),
+            pltpu.VMEM((SLOT, ROWS + 32, LANES), F32),
             pltpu.VMEM((BATCH, 264, LANES), F32),
             pltpu.VMEM((BATCH, 256, LANES), F32),
-            sem((Y - 1,)), sem((Y - 1,)), sem((2, 4)), sem((2, 4)),
+            sem((Y - 1,)), sem((Y - 1,)), sem((8,)), sem((8,)),
             sem((BATCH, GROUPS - 1)), sem((BATCH, GROUPS - 1)), sem(()), sem(()),
         ],
         compiler_params=pltpu.CompilerParams(

time: 57.5 us -> 52.8 us (0.918)
  Pallas kernels: 55.9 us -> 50.6 us
    pallas_call x1, Pallas kernels: 55.9 us -> 50.6 us  [shards(): pl.pallas_call(kernel, out_shape=jax.ShapeDtypeStruct((templates.shape[1]...]
where the time goes in v1:
time: 52.8 us; the launch traced here: 52 us
  Pallas kernels  50.6 us (96%)
  local copies, waits for them, and re-layouts  1.38 us (3%)
    pallas_call x1, Pallas kernels, shards(): pl.pallas_call(kernel, out_shape=jax.ShapeDtypeStruct((templates.shape[1]...  50.6 us
    unnamed x1, local copies, waits for them, and re-layouts  1.38 us

profile of v1, /device:TPU:1, one launch (start us, length us, event | category | flops | bytes accessed | tf_op | source)
XLA Modules:
  0.0 52.0 jit_solution(14891428539423106287)
XLA Ops:
  0.0 50.6 %shard_map.46 = f32[32,256]{1,0:T(8,128)} custom-call(bf16[75,160]{1,0:T(8,128)(2,1)} %w_ref.1, bf16[30,32,400]{2,1,0:T(8,128)(2,1)} %bitcast.1, s32[32,30]{1,0:T(8,128)} %ch_ref.1, s32[32,30]{1,0:T(8,128)} %mv_ref.1), custom_call_target="tpu_custom_call" | custom-call | tf_op jit(solution)/shard_map/pallas_call | solution.py:279
  50.6 1.4 %copy.6 = f32[32,256]{1,0:T(8,128)} copy(f32[32,256]{1,0:T(8,128)} %shard_map.46) | data formatting | bytes 65536

commit v2 on v1

--- a/solution.py
+++ b/solution.py
@@ -18,7 +18,8 @@
 PICK, SLOT = 10, 15
 Z, Y, CHUNK = 8, 4, 5
 GROUPS = 16
-BATCH, EACH = 2, 5
+BATCH, EACH = 3, 4
+PART = GROUPS * 2 * EACH
 
 
 def nt(a, b):
@@ -68,17 +69,17 @@
     grp = chan // CH
     low = jnp.min(grp, axis=1, keepdims=True)
     high = jnp.max(grp, axis=1, keepdims=True)
-    lane = iota((n, BATCH * 256), 1)
-    batch, group, part, row = lane // 256, lane % 256 // 16, lane % 16 // 8, lane % 8
+    lane = iota((n, BATCH * PART), 1)
+    batch, group, part, row = lane // PART, lane % PART // (2 * EACH), lane % (2 * EACH) // EACH, lane % EACH
     here = (group == low) | (group == high)
     rank = nn(ones_where(iota((n, n), 1) < iota((n, n), 0)), ones_where(here)).astype(I32)
-    hit = here & (part == half) & (row < EACH) & (rank == batch * EACH + row)
+    hit = here & (part == half) & (rank == batch * EACH + row)
     return jnp.where(hit, 1.0, 0.0)
 
 
-def kernel(w_ref, t_hbm, ch_ref, mv_ref, o_ref,
-           wide, ybuf, x_all, t_ref, scal_v, scal, units, band, xs, sqs, frames, lev, rolled, outbox, inbox,
-           y_send, y_recv, z_send, z_recv, a_send, a_recv, t_sem, s_sem):
+def kernel(w_hbm, t_hbm, ch_hbm, mv_hbm, o_ref,
+           w_ref, ch_ref, mv_ref, wide, ybuf, x_all, t_ref, scal_v, scal, units, band, xs, sqs, frames, lev, rolled, outbox, inbox,
+           y_send, y_recv, z_send, z_recv, a_send, a_recv, in_sem, s_sem):
     tm, st = lax.axis_index("tmpl"), lax.axis_index("sta")
     zz, yy = tm // Y, tm % Y
     z_peer = {d: (tm + (Z + d) * Y) % (Z * Y) for d in (1, -1, 2, -2)}
@@ -91,15 +92,18 @@
     for p in s_peer:
         pl.semaphore_signal(barrier, inc=1, device_id={"sta": p}, device_id_type=pl.DeviceIdType.MESH)
 
-    t_copy = pltpu.make_async_copy(t_hbm, t_ref, t_sem)
-    t_copy.start()
+    copies = [pltpu.make_async_copy(src, dst, in_sem.at[n]) for n, (src, dst) in enumerate(
+        ((w_hbm, w_ref), (ch_hbm, ch_ref), (mv_hbm, mv_ref), (t_hbm, t_ref)))]
+    for cp in copies:
+        cp.start()
+    outbox[...] = jnp.zeros_like(outbox)
 
     wide[...] = jnp.zeros_like(wide)
+    copies[0].wait()
     wide[pl.ds(0, CH), pl.ds(0, 160)] = w_ref[...].astype(F32)
     own = pltpu.roll(wide[...], 32 * yy, 1)
     own = jnp.concatenate([own[:, :LANES], own[:, LANES:]], axis=0).astype(BF16)
     ybuf[yy] = own
-    outbox[...] = jnp.zeros_like(outbox)
 
     pl.semaphore_wait(barrier, Y - 1 + 4 + GROUPS - 1)
 
@@ -111,6 +115,8 @@
         cp.start()
         y_copies.append(cp)
 
+    copies[1].wait()
+    copies[2].wait()
     sc, place = pair_lists(st * CH, ch_ref[...], mv_ref[...])
     scal_v[...] = sc
     s_copy = pltpu.make_async_copy(scal_v, scal, s_sem)
@@ -125,7 +131,7 @@
             v += parts[n][:CHP]
         if n > 0:
             v += parts[n - 1][CHP:]
-        x_all[n] = v.astype(BF16)
+        x_all[2 * CHUNK + n] = v.astype(BF16)
 
     def pass_on(n, chunk, d, first=0, count=CHUNK):
         there = (chunk - d) % Z
@@ -135,14 +141,14 @@
             send_sem=z_send.at[n], recv_sem=z_recv.at[n],
             device_id={"tmpl": z_peer[d]}, device_id_type=pl.DeviceIdType.MESH)
 
-    from_two = [pass_on(0, 0, 2), pass_on(1, 0, -2)]
-    from_one = [pass_on(2, 0, 1), pass_on(3, 0, -1)]
-    from_four = [pass_on(4, -2, 2, 0, 3), pass_on(5, 2, -2, 3, 2)]
-    from_three = [pass_on(6, -2, 1), pass_on(7, 2, -1)]
+    from_two = [pass_on(0, 2, 2), pass_on(1, 2, -2)]
+    from_one = [pass_on(2, 2, 1), pass_on(3, 2, -1)]
+    from_four = [pass_on(4, 0, 2, 0, 3), pass_on(5, 4, -2, 3, 2)]
+    from_three = [pass_on(6, 0, 1), pass_on(7, 4, -1)]
     for cp in from_two + from_one:
         cp.start()
 
-    t_copy.wait()
+    copies[3].wait()
     s_copy.wait()
 
     slots, count = t_ref.shape[:2]
@@ -181,7 +187,7 @@
     e, d = iota((5 * LANES, LANES), 0), iota((5 * LANES, LANES), 1)
     window = ones_where((e >= d) & (e < d + TAPS))
     factor = 1.0 / math.sqrt(TAPS * 2 * SLOT)
-    many = 10
+    many = 8
 
     def levels(g):
         s = 0.0
@@ -191,52 +197,62 @@
         for n in range(many):
             lev[pl.ds((g + n) * PITCH, CHP), :] = s[n * CHP:(n + 1) * CHP]
 
-    bands(0, 5)
+    def join(c):
+        g = c * CHUNK + CHUNK - 1
+        first, second = x_all[g].astype(F32), x_all[(g + 1) % ROWS].astype(F32)
+        put(g, pltpu.roll(jnp.where(lane < HALF, second, first), HALF, 1), 1)
+
+    def make_frames():
+        @pl.loop(0, CH)
+        def _(c):
+            for h in range(2):
+                for q in range(4):
+                    v = xs[pl.ds(c + (h * (ROWS + 4) + q) * PITCH, ROWS, stride=PITCH), :]
+                    frames[c, pl.ds(h * ROWS, ROWS), pl.ds(q * LANES, LANES)] = v.astype(BF16)
+
+    def scalars(i, j):
+        return [jnp.clip(scal[n, i * 16 + j], 0, top) for n, top in enumerate((CH - 1, 3, LANES - 1))]
+
+    bands(0, 7)
     for near, far, one in zip(from_two, from_four, from_three):
         near.wait_recv()
         far.start()
         one.start()
-    bands(5, PICK)
-    for c in (0, 2, 6):
+    bands(7, PICK)
+    for c in (2, 0, 4):
         take(c)
     for cp in from_one:
         cp.wait_recv()
-    for c in (1, 7):
+    for c in (1, 3):
         take(c)
-    levels(0)
-    levels(30)
+    for c in range(4):
+        join(c)
+    for g in (0, 8):
+        levels(g)
+
     for cp in from_three:
         cp.wait_recv()
-    for c in (3, 5):
+    for c in (5, 7):
         take(c)
     for cp in from_four:
         cp.wait_recv()
-    take(4)
-    for c in range(Z):
-        g = c * CHUNK + CHUNK - 1
-        first, second = x_all[g].astype(F32), x_all[(g + 1) % ROWS].astype(F32)
-        put(g, pltpu.roll(jnp.where(lane < HALF, second, first), HALF, 1), 1)
-    levels(10)
-    levels(20)
-
-    @pl.loop(0, CH)
-    def _(c):
-        for h in range(2):
-            for q in range(4):
-                v = xs[pl.ds(c + (h * (ROWS + 4) + q) * PITCH, ROWS, stride=PITCH), :]
-                frames[c, pl.ds(h * ROWS, ROWS), pl.ds(q * LANES, LANES)] = v.astype(BF16)
-
-    start = (ROWS - CHUNK * zz) % ROWS
+    take(6)
+    for c in range(4, Z):
+        join(c)
+    for g in (16, 24, 32):
+        levels(g)
+    make_frames()
+
+    start = (ROWS + 2 * CHUNK - CHUNK * zz) % ROWS
     lane32 = iota((32, LANES), 1)
 
     def stacks(b):
-        @pl.loop(0, EACH)
+        @pl.loop(0, min(EACH, PICK - b * EACH))
         def _(ii):
             i = b * EACH + ii
             acc = jnp.zeros((32, LANES), F32)
             for j in range(SLOT):
-                p = i * 16 + j
-                c, a, r = (jnp.clip(scal[n, p], 0, top) for n, top in enumerate((CH - 1, 3, LANES - 1)))
+                c, a, r = scalars(i, j)
                 y = nt(frames[c], band[i * SLOT + j])
                 y = jnp.concatenate([y[:ROWS], y[ROWS:]], axis=1)
                 w = pltpu.roll(y * lev[pl.ds(c, ROWS, stride=PITCH), :], (LANES - r) % LANES, 1)
@@ -244,19 +260,19 @@
                 rolled[j, pl.ds(ROWS, 32), :] = w[:32]
                 here, after = rolled[j, pl.ds(start + a, 32), :], rolled[j, pl.ds(start + a + 1, 32), :]
                 acc += jnp.where(lane32 < LANES - r, here, after)
-            outbox[b, pl.ds(ii, 32, stride=8), :] = acc
+            outbox[b, pl.ds(ii, 32, stride=EACH), :] = acc
 
     sends = []
     for b in range(BATCH):
         stacks(b)
         for d in range(1, GROUPS):
             cp = pltpu.make_async_remote_copy(
-                src_ref=outbox.at[b, pl.ds(s_peer[d - 1] * 16, 16)], dst_ref=inbox.at[b, pl.ds(st * 16, 16)],
+                src_ref=outbox.at[b, pl.ds(s_peer[d - 1] * 2 * EACH, 2 * EACH)], dst_ref=inbox.at[b, pl.ds(st * 2 * EACH, 2 * EACH)],
                 send_sem=a_send.at[b, d - 1], recv_sem=a_recv.at[b, d - 1],
                 device_id={"sta": s_peer[d - 1]}, device_id_type=pl.DeviceIdType.MESH)
             cp.start()
             sends.append(cp)
-        inbox[b, pl.ds(st * 16, 16), :] = outbox[b, pl.ds(st * 16, 16), :]
+        inbox[b, pl.ds(st * 2 * EACH, 2 * EACH), :] = outbox[b, pl.ds(st * 2 * EACH, 2 * EACH), :]
 
     hits = [combine_rows(ch_ref[...], h) for h in range(2)]
     total = [0.0, 0.0]
@@ -264,7 +280,7 @@
         for cp in sends[b * (GROUPS - 1):(b + 1) * (GROUPS - 1)]:
             cp.wait_recv()
         for h in range(2):
-            total[h] += jnp.dot(hits[h][:, b * 256:(b + 1) * 256], inbox[b],
+            total[h] += jnp.dot(hits[h][:, b * PART:(b + 1) * PART], inbox[b],
                                 precision=lax.Precision.HIGHEST, preferred_element_type=F32)
     for h in range(2):
         o_ref[:, pl.ds(h * LANES, LANES)] = total[h]
@@ -279,9 +295,12 @@
     return pl.pallas_call(
         kernel,
         out_shape=jax.ShapeDtypeStruct((templates.shape[1], 2 * LANES), F32),
-        in_specs=[vm, pl.BlockSpec(memory_space=pl.ANY), vm, vm],
+        in_specs=[pl.BlockSpec(memory_space=pl.ANY)] * 4,
         out_specs=vm,
         scratch_shapes=[
+            pltpu.VMEM(waveform.shape, BF16),
+            pltpu.VMEM(channel.shape, I32),
+            pltpu.VMEM(moveout.shape, I32),
             pltpu.VMEM((CHP, 2 * LANES), F32),
             pltpu.VMEM((Y, 2 * CHP, LANES), BF16),
             pltpu.VMEM((ROWS, CHP, LANES), BF16),
@@ -292,13 +311,13 @@
             pltpu.VMEM((PICK * SLOT, HALF, WIDE), BF16),
             pltpu.VMEM((2 * (ROWS + 4) * PITCH + CHP, LANES), F32),
             pltpu.VMEM(((ROWS + 4) * CHP, LANES), BF16),
-            pltpu.VMEM((CHP, 2 * ROWS, WIDE), BF16),
+            pltpu.VMEM((CH, 2 * ROWS, WIDE), BF16),
             pltpu.VMEM((ROWS * PITCH + CHP, LANES), F32),
             pltpu.VMEM((SLOT, ROWS + 32, LANES), F32),
-            pltpu.VMEM((BATCH, 264, LANES), F32),
-            pltpu.VMEM((BATCH, 256, LANES), F32),
+            pltpu.VMEM((BATCH, PART + 8, LANES), F32),
+            pltpu.VMEM((BATCH, PART, LANES), F32),
             sem((Y - 1,)), sem((Y - 1,)), sem((8,)), sem((8,)),
-            sem((BATCH, GROUPS - 1)), sem((BATCH, GROUPS - 1)), sem(()), sem(()),
+            sem((BATCH, GROUPS - 1)), sem((BATCH, GROUPS - 1)), sem((4,)), sem(()),
         ],
         compiler_params=pltpu.CompilerParams(
             vmem_limit_bytes=56 << 20, collective_id=0, has_side_effects=True

time: 52.8 us -> 52.2 us (0.989)
  no operation moved by 1% of the time
where the time goes in v2:
time: 52.2 us; the launch traced here: 51.5 us
  Pallas kernels  50.2 us (96%)
  local copies, waits for them, and re-layouts  1.38 us (3%)
    pallas_call x1, Pallas kernels, shards(): pl.pallas_call(kernel, out_shape=jax.ShapeDtypeStruct((templates.shape[1]...  50.2 us
    unnamed x1, local copies, waits for them, and re-layouts  1.38 us

profile of v2, /device:TPU:1, one launch (start us, length us, event | category | flops | bytes accessed | tf_op | source)
XLA Modules:
  0.0 51.5 jit_solution(17736285288753746236)
XLA Ops:
  0.0 50.2 %shard_map.46 = f32[32,256]{1,0:T(8,128)} custom-call(bf16[75,160]{1,0:T(8,128)(2,1)} %w_hbm.1, bf16[30,32,400]{2,1,0:T(8,128)(2,1)} %bitcast.1, s32[32,30]{1,0:T(8,128)} %ch_hbm.1, s32[32,30]{1,0:T(8,128)} %mv_hbm.1), custom_call_target="tpu_custom_call" | custom-call | tf_op jit(solution)/shard_map/pallas_call | solution.py:295
  50.2 1.4 %copy.6 = f32[32,256]{1,0:T(8,128)} copy(f32[32,256]{1,0:T(8,128)} %shard_map.46) | data formatting | bytes 65536

commit v3 on v2

--- a/solution.py
+++ b/solution.py
@@ -13,6 +13,7 @@
 HALF = 64
 WIDE = 512
 CH, CHP = 75, 80
+LOW, HIGH = 64, 16
 PITCH = 84
 ROWS = 40
 PICK, SLOT = 10, 15
@@ -78,11 +79,11 @@
 
 
 def kernel(w_hbm, t_hbm, ch_hbm, mv_hbm, o_ref,
-           w_ref, ch_ref, mv_ref, wide, ybuf, x_all, t_ref, scal_v, scal, units, band, xs, sqs, frames, lev, rolled, outbox, inbox,
-           y_send, y_recv, z_send, z_recv, a_send, a_recv, in_sem, s_sem):
+           w_ref, ch_ref, mv_ref, wide, ybuf, zbuf, x_low, x_high, t_ref, scal_v, scal, units, band, xs, sqs, frames, lev, rolled, outbox, inbox,
+           y_send, y_recv, b_send, b_recv, c_send, c_recv, z_send, z_recv, a_send, a_recv, in_sem, s_sem):
     tm, st = lax.axis_index("tmpl"), lax.axis_index("sta")
     zz, yy = tm // Y, tm % Y
-    z_peer = {d: (tm + (Z + d) * Y) % (Z * Y) for d in (1, -1, 2, -2)}
+    z_peer = {d: (tm + (Z + d) * Y) % (Z * Y) for d in (4, 3, -3, 2, -2, 1, -1)}
     y_peer = [zz * Y + (yy + d) % Y for d in range(1, Y)]
     s_peer = [(st + d) % GROUPS for d in range(1, GROUPS)]
 
@@ -102,10 +103,11 @@
     copies[0].wait()
     wide[pl.ds(0, CH), pl.ds(0, 160)] = w_ref[...].astype(F32)
     own = pltpu.roll(wide[...], 32 * yy, 1)
-    own = jnp.concatenate([own[:, :LANES], own[:, LANES:]], axis=0).astype(BF16)
-    ybuf[yy] = own
-
-    pl.semaphore_wait(barrier, Y - 1 + 4 + GROUPS - 1)
+    one, two = own[:, :LANES].astype(BF16), own[:, LANES:].astype(BF16)
+    ybuf[yy] = jnp.concatenate([one[:LOW], two[:LOW]], axis=0)
+    zbuf[yy, 2] = jnp.concatenate([one[LOW:], two[LOW:]], axis=0)
+
+    pl.semaphore_wait(barrier, Y - 1 + Z - 1 + GROUPS - 1)
 
     y_copies = []
     for d in range(1, Y):
@@ -114,6 +116,14 @@
             device_id={"tmpl": y_peer[d - 1]}, device_id_type=pl.DeviceIdType.MESH)
         cp.start()
         y_copies.append(cp)
+
+    b_copies = []
+    for n, d in enumerate(z_peer):
+        cp = pltpu.make_async_remote_copy(
+            src_ref=zbuf.at[yy, 2], dst_ref=zbuf.at[yy, (2 - d) % Z], send_sem=b_send.at[n], recv_sem=b_recv.at[n],
+            device_id={"tmpl": z_peer[d]}, device_id_type=pl.DeviceIdType.MESH)
+        cp.start()
+        b_copies.append(cp)
 
     copies[1].wait()
     copies[2].wait()
@@ -124,20 +134,20 @@
 
     for cp in y_copies:
         cp.wait()
-    parts = [ybuf[y].astype(F32) for y in range(Y)]
-    for n in range(CHUNK):
-        v = 0.0
-        if n < Y:
-            v += parts[n][:CHP]
-        if n > 0:
-            v += parts[n - 1][CHP:]
-        x_all[2 * CHUNK + n] = v.astype(BF16)
+
+    def blocks(parts, rows):
+        parts = [v.astype(F32) for v in parts]
+        whole = [parts[0][:rows]] + [parts[n][:rows] + parts[n - 1][rows:] for n in range(1, Y)] + [parts[Y - 1][rows:]]
+        return [v.astype(BF16) for v in whole]
+
+    for n, v in enumerate(blocks([ybuf[y] for y in range(Y)], LOW)):
+        x_low[2 * CHUNK + n] = v
 
     def pass_on(n, chunk, d, first=0, count=CHUNK):
         there = (chunk - d) % Z
         return pltpu.make_async_remote_copy(
-            src_ref=x_all.at[pl.ds(chunk % Z * CHUNK + first, count)],
-            dst_ref=x_all.at[pl.ds(there * CHUNK + first, count)],
+            src_ref=x_low.at[pl.ds(chunk % Z * CHUNK + first, count)],
+            dst_ref=x_low.at[pl.ds(there * CHUNK + first, count)],
             send_sem=z_send.at[n], recv_sem=z_recv.at[n],
             device_id={"tmpl": z_peer[d]}, device_id_type=pl.DeviceIdType.MESH)
 
@@ -147,6 +157,16 @@
     from_three = [pass_on(6, 0, 1), pass_on(7, 4, -1)]
     for cp in from_two + from_one:
         cp.start()
+
+    c_copies = []
+    for cp in b_copies:
+        cp.wait_recv()
+    for d in range(1, Y):
+        cp = pltpu.make_async_remote_copy(
+            src_ref=zbuf.at[yy], dst_ref=zbuf.at[yy], send_sem=c_send.at[d - 1], recv_sem=c_recv.at[d - 1],
+            device_id={"tmpl": y_peer[d - 1]}, device_id_type=pl.DeviceIdType.MESH)
+        cp.start()
+        c_copies.append(cp)
 
     copies[3].wait()
     s_copy.wait()
@@ -171,8 +191,11 @@
     def put(g, row, odd):
         xs[pl.ds((g + odd * (ROWS + 4)) * PITCH, CHP), :] = row
 
+    def block(g):
+        return jnp.concatenate([x_low[g].astype(F32), x_high[g].astype(F32)], axis=0)
+
     def take(c):
-        rows = [x_all[c * CHUNK + n].astype(F32) for n in range(CHUNK)]
+        rows = [block(c * CHUNK + n) for n in range(CHUNK)]
         for n in range(CHUNK):
             again = (0, ROWS) if c == 0 and n < 4 else (0,)
             later = pltpu.roll(jnp.where(lane < HALF, rows[n + 1], rows[n]), HALF, 1) if n < CHUNK - 1 else None
@@ -199,7 +222,7 @@
 
     def join(c):
         g = c * CHUNK + CHUNK - 1
-        first, second = x_all[g].astype(F32), x_all[(g + 1) % ROWS].astype(F32)
+        first, second = block(g), block((g + 1) % ROWS)
         put(g, pltpu.roll(jnp.where(lane < HALF, second, first), HALF, 1), 1)
 
     def make_frames():
@@ -216,9 +239,14 @@
     bands(0, 7)
     for near, far, one in zip(from_two, from_four, from_three):
         near.wait_recv()
+        one.start()
         far.start()
-        one.start()
     bands(7, PICK)
+    for cp in c_copies:
+        cp.wait_recv()
+    for c in range(Z):
+        for n, v in enumerate(blocks([zbuf[y, c] for y in range(Y)], HIGH)):
+            x_high[c * CHUNK + n] = v
     for c in (2, 0, 4):
         take(c)
     for cp in from_one:
@@ -284,7 +312,7 @@
                                 precision=lax.Precision.HIGHEST, preferred_element_type=F32)
     for h in range(2):
         o_ref[:, pl.ds(h * LANES, LANES)] = total[h]
-    for cp in from_two + from_one + from_four + from_three + sends:
+    for cp in b_copies + c_copies + from_two + from_one + from_four + from_three + sends:
         cp.wait_send()
 
 
@@ -302,8 +330,10 @@
             pltpu.VMEM(channel.shape, I32),
             pltpu.VMEM(moveout.shape, I32),
             pltpu.VMEM((CHP, 2 * LANES), F32),
-            pltpu.VMEM((Y, 2 * CHP, LANES), BF16),
-            pltpu.VMEM((ROWS, CHP, LANES), BF16),
+            pltpu.VMEM((Y, 2 * LOW, LANES), BF16),
+            pltpu.VMEM((Y, Z, 2 * HIGH, LANES), BF16),
+            pltpu.VMEM((ROWS, LOW, LANES), BF16),
+            pltpu.VMEM((ROWS, HIGH, LANES), BF16),
             pltpu.VMEM(templates.shape, BF16),
             pltpu.VMEM((8, 256), I32),
             pltpu.SMEM((8, 256), I32),
@@ -316,7 +346,7 @@
             pltpu.VMEM((SLOT, ROWS + 32, LANES), F32),
             pltpu.VMEM((BATCH, PART + 8, LANES), F32),
             pltpu.VMEM((BATCH, PART, LANES), F32),
-            sem((Y - 1,)), sem((Y - 1,)), sem((8,)), sem((8,)),
+            sem((Y - 1,)), sem((Y - 1,)), sem((Z - 1,)), sem((Z - 1,)), sem((Y - 1,)), sem((Y - 1,)), sem((8,)), sem((8,)),
             sem((BATCH, GROUPS - 1)), sem((BATCH, GROUPS - 1)), sem((4,)), sem(()),
         ],
         compiler_params=pltpu.CompilerParams(

time: 52.2 us -> 49.3 us (0.944)
  Pallas kernels: 50.2 us -> 47.8 us
    pallas_call x1, Pallas kernels: 50.2 us -> 47.8 us  [shards(): pl.pallas_call(kernel, out_shape=jax.ShapeDtypeStruct((templates.shape[1]...]
where the time goes in v3:
time: 49.3 us; the launch traced here: 49.1 us
  Pallas kernels  47.8 us (97%)
  local copies, waits for them, and re-layouts  1.38 us (3%)
    pallas_call x1, Pallas kernels, shards(): pl.pallas_call(kernel, out_shape=jax.ShapeDtypeStruct((templates.shape[1]...  47.8 us
    unnamed x1, local copies, waits for them, and re-layouts  1.38 us

profile of v3, /device:TPU:1, one launch (start us, length us, event | category | flops | bytes accessed | tf_op | source)
XLA Modules:
  0.0 49.1 jit_solution(7196427456137834524)
XLA Ops:
  0.0 47.8 %shard_map.46 = f32[32,256]{1,0:T(8,128)} custom-call(bf16[75,160]{1,0:T(8,128)(2,1)} %w_hbm.1, bf16[30,32,400]{2,1,0:T(8,128)(2,1)} %bitcast.1, s32[32,30]{1,0:T(8,128)} %ch_hbm.1, s32[32,30]{1,0:T(8,128)} %mv_hbm.1), custom_call_target="tpu_custom_call" | custom-call | tf_op jit(solution)/shard_map/pallas_call | solution.py:323
  47.8 1.4 %copy.6 = f32[32,256]{1,0:T(8,128)} copy(f32[32,256]{1,0:T(8,128)} %shard_map.46) | data formatting | bytes 65536

commit v4 on v3

--- a/solution.py
+++ b/solution.py
@@ -16,6 +16,7 @@
 LOW, HIGH = 64, 16
 PITCH = 84
 ROWS = 40
+EARLY = 16
 PICK, SLOT = 10, 15
 Z, Y, CHUNK = 8, 4, 5
 GROUPS = 16
@@ -225,13 +226,15 @@
         first, second = block(g), block((g + 1) % ROWS)
         put(g, pltpu.roll(jnp.where(lane < HALF, second, first), HALF, 1), 1)
 
-    def make_frames():
-        @pl.loop(0, CH)
-        def _(c):
-            for h in range(2):
-                for q in range(4):
-                    v = xs[pl.ds(c + (h * (ROWS + 4) + q) * PITCH, ROWS, stride=PITCH), :]
-                    frames[c, pl.ds(h * ROWS, ROWS), pl.ds(q * LANES, LANES)] = v.astype(BF16)
+    def make_frames(first, count):
+        @pl.loop(0, CH // 5)
+        def _(c5):
+            for u in range(5):
+                c = c5 * 5 + u
+                for h in range(2):
+                    for q in range(4):
+                        v = xs[pl.ds(c + (h * (ROWS + 4) + q + first) * PITCH, count, stride=PITCH), :]
+                        frames[c, pl.ds(2 * first + h * count, count), pl.ds(q * LANES, LANES)] = v.astype(BF16)
 
     def scalars(i, j):
         return [jnp.clip(scal[n, i * 16 + j], 0, top) for n, top in enumerate((CH - 1, 3, LANES - 1))]
@@ -257,6 +260,7 @@
         join(c)
     for g in (0, 8):
         levels(g)
+    make_frames(0, EARLY)
 
     for cp in from_three:
         cp.wait_recv()
@@ -269,26 +273,30 @@
         join(c)
     for g in (16, 24, 32):
         levels(g)
-    make_frames()
+    make_frames(EARLY, ROWS - EARLY)
 
     start = (ROWS + 2 * CHUNK - CHUNK * zz) % ROWS
     lane32 = iota((32, LANES), 1)
 
     def stacks(b):
-        @pl.loop(0, min(EACH, PICK - b * EACH))
-        def _(ii):
-            i = b * EACH + ii
-            acc = jnp.zeros((32, LANES), F32)
-            for j in range(SLOT):
-                c, a, r = scalars(i, j)
-                y = nt(frames[c], band[i * SLOT + j])
-                y = jnp.concatenate([y[:ROWS], y[ROWS:]], axis=1)
-                w = pltpu.roll(y * lev[pl.ds(c, ROWS, stride=PITCH), :], (LANES - r) % LANES, 1)
-                rolled[j, pl.ds(0, ROWS), :] = w
-                rolled[j, pl.ds(ROWS, 32), :] = w[:32]
-                here, after = rolled[j, pl.ds(start + a, 32), :], rolled[j, pl.ds(start + a + 1, 32), :]
-                acc += jnp.where(lane32 < LANES - r, here, after)
-            outbox[b, pl.ds(ii, 32, stride=EACH), :] = acc
+        @pl.loop(0, min(EACH, PICK - b * EACH) // 2)
+        def _(some):
+            for u in range(2):
+                i = b * EACH + some * 2 + u
+                acc = jnp.zeros((32, LANES), F32)
+                for j in range(SLOT):
+                    c, a, r = scalars(i, j)
+                    y = nt(frames[c], band[i * SLOT + j])
+                    even = jnp.concatenate([y[:EARLY], y[2 * EARLY:ROWS + EARLY]], axis=0)
+                    odd = jnp.concatenate([y[EARLY:2 * EARLY], y[ROWS + EARLY:]], axis=0)
+                    y = jnp.concatenate([even, odd], axis=1)
+                    w = pltpu.roll(y * lev[pl.ds(c, ROWS, stride=PITCH), :], (LANES - r) % LANES, 1)
+                    n = u * SLOT + j
+                    rolled[n, pl.ds(0, ROWS), :] = w
+                    rolled[n, pl.ds(ROWS, 32), :] = w[:32]
+                    here, after = rolled[n, pl.ds(start + a, 32), :], rolled[n, pl.ds(start + a + 1, 32), :]
+                    acc += jnp.where(lane32 < LANES - r, here, after)
+                outbox[b, pl.ds(some * 2 + u, 32, stride=EACH), :] = acc
 
     sends = []
     for b in range(BATCH):
@@ -343,7 +351,7 @@
             pltpu.VMEM(((ROWS + 4) * CHP, LANES), BF16),
             pltpu.VMEM((CH, 2 * ROWS, WIDE), BF16),
             pltpu.VMEM((ROWS * PITCH + CHP, LANES), F32),
-            pltpu.VMEM((SLOT, ROWS + 32, LANES), F32),
+            pltpu.VMEM((2 * SLOT, ROWS + 32, LANES), F32),
             pltpu.VMEM((BATCH, PART + 8, LANES), F32),
             pltpu.VMEM((BATCH, PART, LANES), F32),
             sem((Y - 1,)), sem((Y - 1,)), sem((Z - 1,)), sem((Z - 1,)), sem((Y - 1,)), sem((Y - 1,)), sem((8,)), sem((8,)),

time: 49.3 us -> 46.9 us (0.951)
  Pallas kernels: 47.8 us -> 45.3 us
    pallas_call x1, Pallas kernels: 47.8 us -> 45.3 us  [shards(): pl.pallas_call(kernel, out_shape=jax.ShapeDtypeStruct((templates.shape[1]...]
where the time goes in v4:
time: 46.9 us; the launch traced here: 46.7 us
  Pallas kernels  45.3 us (97%)
  local copies, waits for them, and re-layouts  1.38 us (3%)
    pallas_call x1, Pallas kernels, shards(): pl.pallas_call(kernel, out_shape=jax.ShapeDtypeStruct((templates.shape[1]...  45.3 us
    unnamed x1, local copies, waits for them, and re-layouts  1.38 us

profile of v4, /device:TPU:1, one launch (start us, length us, event | category | flops | bytes accessed | tf_op | source)
XLA Modules:
  0.0 46.7 jit_solution(2965843440346630359)
XLA Ops:
  0.0 45.3 %shard_map.46 = f32[32,256]{1,0:T(8,128)} custom-call(bf16[75,160]{1,0:T(8,128)(2,1)} %w_hbm.1, bf16[30,32,400]{2,1,0:T(8,128)(2,1)} %bitcast.1, s32[32,30]{1,0:T(8,128)} %ch_hbm.1, s32[32,30]{1,0:T(8,128)} %mv_hbm.1), custom_call_target="tpu_custom_call" | custom-call | tf_op jit(solution)/shard_map/pallas_call | solution.py:331
  45.3 1.4 %copy.6 = f32[32,256]{1,0:T(8,128)} copy(f32[32,256]{1,0:T(8,128)} %shard_map.46) | data formatting | bytes 65536

commit v5 on v4

--- a/solution.py
+++ b/solution.py
@@ -279,10 +279,12 @@
     lane32 = iota((32, LANES), 1)
 
     def stacks(b):
-        @pl.loop(0, min(EACH, PICK - b * EACH) // 2)
+        size = min(EACH, PICK - b * EACH)
+
+        @pl.loop(0, 1)
         def _(some):
-            for u in range(2):
-                i = b * EACH + some * 2 + u
+            for u in range(size):
+                i = b * EACH + some * size + u
                 acc = jnp.zeros((32, LANES), F32)
                 for j in range(SLOT):
                     c, a, r = scalars(i, j)
@@ -296,7 +298,7 @@
                     rolled[n, pl.ds(ROWS, 32), :] = w[:32]
                     here, after = rolled[n, pl.ds(start + a, 32), :], rolled[n, pl.ds(start + a + 1, 32), :]
                     acc += jnp.where(lane32 < LANES - r, here, after)
-                outbox[b, pl.ds(some * 2 + u, 32, stride=EACH), :] = acc
+                outbox[b, pl.ds(some * size + u, 32, stride=EACH), :] = acc
 
     sends = []
     for b in range(BATCH):
@@ -351,7 +353,7 @@
             pltpu.VMEM(((ROWS + 4) * CHP, LANES), BF16),
             pltpu.VMEM((CH, 2 * ROWS, WIDE), BF16),
             pltpu.VMEM((ROWS * PITCH + CHP, LANES), F32),
-            pltpu.VMEM((2 * SLOT, ROWS + 32, LANES), F32),
+            pltpu.VMEM((4 * SLOT, ROWS + 32, LANES), F32),
             pltpu.VMEM((BATCH, PART + 8, LANES), F32),
             pltpu.VMEM((BATCH, PART, LANES), F32),
             sem((Y - 1,)), sem((Y - 1,)), sem((Z - 1,)), sem((Z - 1,)), sem((Y - 1,)), sem((Y - 1,)), sem((8,)), sem((8,)),

time: 46.9 us -> 46.5 us (level)
  no operation moved by 1% of the time
where the time goes in v5:
time: 46.5 us; the launch traced here: 46.3 us
  Pallas kernels  44.9 us (97%)
  local copies, waits for them, and re-layouts  1.38 us (3%)
    pallas_call x1, Pallas kernels, shards(): pl.pallas_call(kernel, out_shape=jax.ShapeDtypeStruct((templates.shape[1]...  44.9 us
    unnamed x1, local copies, waits for them, and re-layouts  1.38 us

profile of v5, /device:TPU:1, one launch (start us, length us, event | category | flops | bytes accessed | tf_op | source)
XLA Modules:
  0.0 46.3 jit_solution(10523954420521618594)
XLA Ops:
  0.0 44.9 %shard_map.46 = f32[32,256]{1,0:T(8,128)} custom-call(bf16[75,160]{1,0:T(8,128)(2,1)} %w_hbm.1, bf16[30,32,400]{2,1,0:T(8,128)(2,1)} %bitcast.1, s32[32,30]{1,0:T(8,128)} %ch_hbm.1, s32[32,30]{1,0:T(8,128)} %mv_hbm.1), custom_call_target="tpu_custom_call" | custom-call | tf_op jit(solution)/shard_map/pallas_call | solution.py:333
  44.9 1.4 %copy.6 = f32[32,256]{1,0:T(8,128)} copy(f32[32,256]{1,0:T(8,128)} %shard_map.46) | data formatting | bytes 65536
